TPU v7x, 32 devices: a whole 2x2x4 slice. The times are simulated.
32 devices in a mesh: lon: 8 (over y, x, core), lat: 4 (over z).
Axes of the slice: x: 2, y: 2, z: 4, core: 2. Of those that a mesh axis runs over, the one named last changes fastest.
Arguments:
- heat_content_field: float32 [12, 384, 1024], P(None, 'lat', 'lon'), may hold values from -6 to 6
- saltiness_field: float32 [12, 384, 1024], P(None, 'lat', 'lon'), may hold values from -6 to 6
- eastward_cfl_number: float32 [12, 384, 1024], P(None, 'lat', 'lon'), may hold values from -0.4 to 0.4
- northward_cfl_number: float32 [12, 384, 1024], P(None, 'lat', 'lon'), may hold values from -0.4 to 0.4
- seawater_indicator: int32 [384, 1024], P('lat', 'lon'), may hold values 0 or 1
- submerged_layer_total: int32 [384, 1024], P('lat', 'lon'), may hold values from 1 to 12
- seam_partner_index: int32 [1024], replicated, may hold values from 0 to 1023, as said below
Outputs:
- new_temperature: float32 [12, 384, 1024], P(None, 'lat', 'lon')
- new_salinity: float32 [12, 384, 1024], P(None, 'lat', 'lon')
Inputs may be any that keep to these rules, and one draw needn't show every extreme that they name: Each column appears once; the map is a reflection of the columns about a pivot, seam_partner_index[i] = (s - i) mod 1024.
All inputs are finite; a program needn't handle non-finite values. No bound on the sum of `seawater_indicator` on one device may be relied on, other than what follows from the above.
Results may differ from a plain program's by a relative error of at most 0.0003.
Values sent between devices are 32-bit elements; how exact they have to be, the bound alone decides.
No kernel may reach another device: no remote copies, remote signals or barrier semaphores. Data moves between devices by JAX's collectives and lax.ppermute only.
A program may use at most 192 MiB of HBM per device.

v0:
```python
from functools import reduce

import jax
import jax.numpy as jnp
from jax import lax
from jax.sharding import PartitionSpec as P

RATIO_FLOOR = 0.05
SLOPE_FLOOR = 0.5
SLOPE_LIMIT = 2.0
DIFFUSIVITY = 0.1
THERMAL_COEF = 0.2
HALINE_COEF = 0.8
STATE_SIGNS = (1.0, 1.0, -1.0, -1.0, 1.0)


def extended(cells, sides, width, closed):
    for axis, dim in sides:
        count = lax.axis_size(axis)
        ends = count if closed else count - 1
        head = lax.slice_in_dim(cells, 0, width, axis=dim)
        tail = lax.slice_in_dim(cells, cells.shape[dim] - width, cells.shape[dim], axis=dim)
        cells = jnp.concatenate(
            [
                lax.ppermute(tail, axis, [(i, (i + 1) % count) for i in range(ends)]),
                cells,
                lax.ppermute(head, axis, [((i + 1) % count, i) for i in range(ends)]),
            ],
            axis=dim,
        )
    return cells


def sign_column(values):
    return jnp.array(values, jnp.float32).reshape(len(values), 1, 1, 1)


def sided(core, west_col, east_col, south_row, north_row):
    width = core.shape[-1]
    height = core.shape[-2]
    lane = lax.broadcasted_iota(jnp.int32, core.shape, core.ndim - 1)
    level = lax.broadcasted_iota(jnp.int32, core.shape, core.ndim - 2)
    at_east = jnp.where(lane == width - 1, east_col, jnp.roll(core, -1, axis=-1))
    at_west = jnp.where(lane == 0, west_col, jnp.roll(core, 1, axis=-1))
    at_north = jnp.where(level == height - 1, north_row, jnp.roll(core, -1, axis=-2))
    at_south = jnp.where(level == 0, south_row, jnp.roll(core, 1, axis=-2))
    return (core, at_east, at_west, at_north, at_south)


def low_order(tracer, zonal, meridional, wet_sides):
    value_centre, value_east, value_west, value_north, value_south = tracer
    speed_centre, speed_west = (zonal[0], zonal[2])
    flow_centre, flow_south = (meridional[0], meridional[4])
    wet_centre, wet_east, wet_west, wet_north, wet_south = wet_sides
    face_east = wet_centre * wet_east
    face_west = wet_west * wet_centre
    face_north = wet_centre * wet_north
    face_south = wet_south * wet_centre
    upwind_east = face_east * (
        jnp.maximum(speed_centre, 0.0) * value_centre + jnp.minimum(speed_centre, 0.0) * value_east
    )
    upwind_west = face_west * (
        jnp.maximum(speed_west, 0.0) * value_west + jnp.minimum(speed_west, 0.0) * value_centre
    )
    upwind_north = face_north * (
        jnp.maximum(flow_centre, 0.0) * value_centre + jnp.minimum(flow_centre, 0.0) * value_north
    )
    upwind_south = face_south * (
        jnp.maximum(flow_south, 0.0) * value_south + jnp.minimum(flow_south, 0.0) * value_centre
    )
    anti_east = face_east * speed_centre * (value_centre + value_east) * 0.5 - upwind_east
    anti_west = face_west * speed_west * (value_west + value_centre) * 0.5 - upwind_west
    anti_north = face_north * flow_centre * (value_centre + value_north) * 0.5 - upwind_north
    anti_south = face_south * flow_south * (value_south + value_centre) * 0.5 - upwind_south
    upwind = value_centre - wet_centre * (upwind_east - upwind_west + upwind_north - upwind_south)
    inflow = (
        jnp.maximum(anti_west, 0.0)
        - jnp.minimum(anti_east, 0.0)
        + jnp.maximum(anti_south, 0.0)
        - jnp.minimum(anti_north, 0.0)
    )
    outflow = (
        jnp.maximum(anti_east, 0.0)
        - jnp.minimum(anti_west, 0.0)
        + jnp.maximum(anti_north, 0.0)
        - jnp.minimum(anti_south, 0.0)
    )
    anti = (anti_east, anti_west, anti_north, anti_south)
    return (upwind, anti, inflow, outflow)


def ratios(upwind_sides, wet_sides, inflow, outflow):
    value_centre, value_east, value_west, value_north, value_south = upwind_sides
    _, wet_east, wet_west, wet_north, wet_south = wet_sides
    pairs = (
        (value_east, wet_east),
        (value_west, wet_west),
        (value_north, wet_north),
        (value_south, wet_south),
    )
    candidates = [value_centre] + [
        jnp.where(beside_wet > 0.5, beside, value_centre) for beside, beside_wet in pairs
    ]
    highest = reduce(jnp.maximum, candidates)
    lowest = reduce(jnp.minimum, candidates)
    ratio_plus = jnp.minimum(1.0, (highest - value_centre) / jnp.maximum(inflow, RATIO_FLOOR))
    ratio_minus = jnp.minimum(1.0, (value_centre - lowest) / jnp.maximum(outflow, RATIO_FLOOR))
    return jnp.concatenate([ratio_plus, ratio_minus], axis=0)


def limited(ratio_sides, upwind, anti, wet_centre):
    plus_centre, plus_east, plus_west, plus_north, plus_south = [side[:2] for side in ratio_sides]
    minus_centre, minus_east, minus_west, minus_north, minus_south = [
        side[2:] for side in ratio_sides
    ]
    anti_east, anti_west, anti_north, anti_south = anti
    coef_east = jnp.where(
        anti_east >= 0.0, jnp.minimum(plus_east, minus_centre), jnp.minimum(plus_centre, minus_east)
    )
    coef_west = jnp.where(
        anti_west >= 0.0, jnp.minimum(plus_centre, minus_west), jnp.minimum(plus_west, minus_centre)
    )
    coef_north = jnp.where(
        anti_north >= 0.0,
        jnp.minimum(plus_north, minus_centre),
        jnp.minimum(plus_centre, minus_north),
    )
    coef_south = jnp.where(
        anti_south >= 0.0,
        jnp.minimum(plus_centre, minus_south),
        jnp.minimum(plus_south, minus_centre),
    )
    return upwind - wet_centre * (
        coef_east * anti_east
        - coef_west * anti_west
        + coef_north * anti_north
        - coef_south * anti_south
    )


def vertical_of(tracer, wet):
    stacked_wet = wet[:-1] * wet[1:]
    vertical = (tracer[:, 1:] - tracer[:, :-1]) * stacked_wet
    return jnp.concatenate([vertical, jnp.zeros_like(tracer[:, :1])], axis=1)


def isopycnal(values, wet_sides):
    verticals = tuple((vertical_of(tracer, wet) for tracer, wet in zip(values, wet_sides)))
    densities = tuple((HALINE_COEF * tracer[1] - THERMAL_COEF * tracer[0] for tracer in values))
    stratas = tuple(
        (HALINE_COEF * vertical[1] - THERMAL_COEF * vertical[0] for vertical in verticals)
    )

    def face_flux(first, second):
        face = wet_sides[first] * wet_sides[second]
        slope = jnp.clip(
            (densities[second] - densities[first])
            / jnp.maximum(0.5 * (stratas[first] + stratas[second]), SLOPE_FLOOR),
            -SLOPE_LIMIT,
            SLOPE_LIMIT,
        )
        return (
            DIFFUSIVITY
            * face
            * (
                values[second]
                - values[first]
                - slope * 0.5 * (verticals[first] + verticals[second])
            )
        )

    east_flux = face_flux(0, 1)
    west_flux = face_flux(2, 0)
    north_flux = face_flux(0, 3)
    south_flux = face_flux(4, 0)
    return values[0] + wet_sides[0] * (east_flux - west_flux + north_flux - south_flux)


def advance(state, sides):
    state_sides = sides(state, sign_column(STATE_SIGNS), 0)
    tracer = tuple((side[:2] for side in state_sides))
    zonal = tuple((side[2] for side in state_sides))
    meridional = tuple((side[3] for side in state_sides))
    wet_sides = tuple((side[4] for side in state_sides))
    upwind, anti, inflow, outflow = low_order(tracer, zonal, meridional, wet_sides)
    upwind_sides = sides(upwind, sign_column((1.0, 1.0)), 1)
    ratio = ratios(upwind_sides, wet_sides, inflow, outflow)
    ratio_sides = sides(ratio, sign_column((1.0, 1.0, 1.0, 1.0)), 2)
    advected = limited(ratio_sides, upwind, anti, wet_sides[0])
    advected_sides = sides(advected, sign_column((1.0, 1.0)), 3)
    return isopycnal(advected_sides, wet_sides)


def local(
    heat_content_field,
    saltiness_field,
    eastward_cfl_number,
    northward_cfl_number,
    seawater_indicator,
    submerged_layer_total,
    seam_partner_index,
):
    span = heat_content_field.shape[2]
    anchor = lax.axis_index("lon") * span
    on_top = lax.axis_index("lat") == lax.axis_size("lat") - 1
    vertical_layer = jnp.arange(heat_content_field.shape[0], dtype=jnp.int32)[:, None, None]
    submerged_indicator = (
        (seawater_indicator[None] == 1) & (vertical_layer < submerged_layer_total[None])
    ).astype(jnp.float32)
    state = jnp.stack(
        [
            heat_content_field,
            saltiness_field,
            eastward_cfl_number,
            northward_cfl_number,
            submerged_indicator,
        ]
    )
    own_columns = anchor + jnp.arange(span, dtype=jnp.int32)
    facing = jnp.take(seam_partner_index, own_columns)

    def rim_sides(stack, fold_row):
        columns = jnp.concatenate([stack[..., :1], stack[..., -1:]], axis=3)
        column_rim = extended(columns, (("lon", 3),), 1, True)
        rows = jnp.concatenate([stack[:, :, :1, :], stack[:, :, -1:, :]], axis=2)
        row_rim = extended(rows, (("lat", 2),), 1, False)
        north_row = jnp.where(on_top, fold_row, row_rim[:, :, 3:4, :])
        return sided(
            stack, column_rim[..., 0:1], column_rim[..., 3:4], row_rim[:, :, 0:1, :], north_row
        )

    def device_sides(stack, signs, segment):
        top_row = lax.all_gather(stack[:, :, -1:, :], "lon", axis=3, tiled=True)
        fold_row = jnp.take(top_row, facing, axis=3) * signs
        return rim_sides(stack, fold_row)

    final = advance(state, device_sides)
    return (final[0], final[1])


def solution(mesh):
    in_specs = (
        P(None, "lat", "lon"),
        P(None, "lat", "lon"),
        P(None, "lat", "lon"),
        P(None, "lat", "lon"),
        P("lat", "lon"),
        P("lat", "lon"),
        P(),
    )
    out_specs = (P(None, "lat", "lon"), P(None, "lat", "lon"))
    return jax.shard_map(local, mesh=mesh, in_specs=in_specs, out_specs=out_specs, check_vma=False)
```

profile of v0, /device:TPU:0, one launch (start us, length us, event | category | flops | bytes accessed | tf_op | source)
XLA Modules:
  0.0 228.0 jit_solution(16075690337887612869)
XLA Ops:
  5.9 6.2 %collective-permute-start.3 = (f32[5,12,1,128]{3,2,1,0:T(1,128)}, f32[5,12,1,128]{3,2,1,0:T(1,128)}, u32[]{:S(2)}, u32[]{:S(2)}) collective-permute-start(f32[5,12,1,128]{3,2,1,0:T(1,128)} %get-tuple-element.46), channel_id=1, source_target_pairs={{0,1},{1,2},{2,3},{4,5},{5,6},{6,7},{8,9},{9,10},{10,11},{12,13},{... | collective-permute-start | bytes 92168 | tf_op jit(solution)/shard_map/ppermute | solution.py:25
  12.1 3.7 %fusion.105 = (f32[5,12,96,1]{3,2,1,0:T(8,128)}, f32[5,12,96,1]{3,2,1,0:T(8,128)}) fusion(f32[5,12,96,128]{3,2,1,0:T(8,128)S(1)} %convert_dynamic-update-slice_fusion), kind=kLoop, calls=%fused_computation.255 | loop fusion | bytes 92160 | tf_op jit(solution)/shard_map/slice | solution.py:223
  15.8 2.9 %copy.952 = f32[5,12,96,1]{2,3,1,0:T(1,128)} copy(f32[5,12,96,1]{3,2,1,0:T(8,128)} %get-tuple-element.41) | data formatting | bytes 46080 | tf_op jit(solution)/shard_map/slice | solution.py:223
  20.4 2.9 %copy.953 = f32[5,12,96,1]{2,3,1,0:T(1,128)} copy(f32[5,12,96,1]{3,2,1,0:T(8,128)} %get-tuple-element.42) | data formatting | bytes 46080 | tf_op jit(solution)/shard_map/slice | solution.py:223
  24.9 3.0 %fusion.106 = (f32[5,12,95,128]{3,2,1,0:T(8,128)}, f32[5,12,95,128]{3,2,1,0:T(8,128)}) fusion(f32[5,12,96,128]{3,2,1,0:T(8,128)S(1)} %convert_dynamic-update-slice_fusion), kind=kLoop, calls=%fused_computation.256 | loop fusion | bytes 11673600 | tf_op jit(solution)/shard_map/jit(_roll_static)/slice | solution.py:45
  28.5 3.6 %fusion.104 = (f32[5,12,96,127]{3,2,1,0:T(8,128)}, f32[5,12,96,127]{3,2,1,0:T(8,128)}) fusion(f32[5,12,96,128]{3,2,1,0:T(8,128)S(1)} %convert_dynamic-update-slice_fusion), kind=kLoop, calls=%fused_computation.254 | loop fusion | bytes 11704320 | tf_op jit(solution)/shard_map/jit(_roll_static)/slice | solution.py:43
  35.0 11.3 %all_gather.12 = f32[5,12,1,1024]{3,2,1,0:T(1,128)} all-gather(f32[5,12,1,128]{3,2,1,0:T(1,128)} %get-tuple-element.46), channel_id=1, replica_groups=mesh['lon'=8,'lat'=4] {'lon'}, dimensions={3}, use_global_device_ids=true | all-gather | bytes 276480 | tf_op jit(solution)/shard_map/all_gather | solution.py:233
  46.3 3.8 %copy.954 = f32[5,12,1,1024]{1,0,3,2:T(8,128)} copy(f32[5,12,1,1024]{3,2,1,0:T(1,128)} %all_gather.12) | data formatting | bytes 491520 | tf_op jit(solution)/shard_map/all_gather | solution.py:233
  50.1 3.7 %gather_fusion.1 = f32[128,5,12]{2,1,0:T(8,128)} fusion(f32[5,12,1024]{1,0,2:T(8,128)} %bitcast.132, s32[1024]{0:T(1024)} %pad_clamp_fusion.1), kind=kCustom, calls=%fused_computation.3 | custom fusion | bytes 61952 | tf_op jit(solution)/shard_map/jit(_take)/gather | solution.py:234
  56.4 3.2 %maximum_select_fusion = f32[5,12,96,128]{3,2,1,0:T(8,128)S(1)} fusion(f32[5,12,96,1]{3,2,1,0:T(8,128)S(1)} %copy-done.5, f32[5,12,96,127]{3,2,1,0:T(8,128)} %get-tuple-element.39, f32[5,12,96]{2,1,0:T(8,128)S(1)} %bitcast.143, pred[128]{0:T(512)(128)(4,1)} %get-tuple-element.98), kind=kLoop, calls=%fused_computation.19 | loop fusion | flops 1474560 | bytes 5921408 | tf_op jit(solution)/shard_map/jit(_where)/select_n | solution.py:43
  69.7 2.4 %copy.1012 = f32[5,12,1,128]{3,1,2,0:T(8,128)S(1)} copy(f32[5,12,1,128]{3,2,1,0:T(1,128)} %collective-permute-done.3) | data formatting | bytes 61440
  73.7 2.2 multiply_bitcast_fusion.7
  83.6 3.5 %collective-permute-start.7 = (f32[2,12,1,128]{3,2,1,0:T(1,128)S(1)}, f32[2,12,1,128]{3,2,1,0:T(1,128)}, u32[]{:S(2)}, u32[]{:S(2)}) collective-permute-start(f32[2,12,1,128]{3,2,1,0:T(1,128)S(1)} %get-tuple-element.72), channel_id=1, source_target_pairs={{0,1},{1,2},{2,3},{4,5},{5,6},{6,7},{8,9},{9,10},{10,11},{12,13},{... | collective-permute-start | bytes 36872 | tf_op jit(solution)/shard_map/ppermute | solution.py:25
  94.0 9.3 %all_gather.13 = f32[2,12,1,1024]{3,0,2,1:T(2,128)S(1)} all-gather(f32[2,12,1,128]{3,0,2,1:T(2,128)} %copy.960), channel_id=1, replica_groups=mesh['lon'=8,'lat'=4] {'lon'}, dimensions={3}, use_global_device_ids=true | all-gather | bytes 110592 | tf_op jit(solution)/shard_map/all_gather | solution.py:233
  107.9 10.3 %fusion.12 = (f32[2,12,96,128]{3,2,1,0:T(8,128)S(1)}, f32[2,12,96,128]{3,2,1,0:T(8,128)S(1)}, f32[2,12,96,128]{3,2,1,0:T(8,128)S(1)}, f32[2,12,96,128]{3,2,1,0:T(8,128)S(1)}, f32[2,12,96,128]{3,2,1,0:T(8,128)S(1)}) fusion(f32[2,12,96,128]{3,2,1,0:T(8,128)S(1)} %multiply_subtract_fusion.4, f32[2,12,1,128]{3,2,1,0:T(1,128)} %get-tuple-element.73, ...), kind=kLoop, calls=%fused_computation.41 | loop fusion | flops 17694720 | bytes 27765184 | tf_op jit(solution)/shard_map/min | solution.py:106
  118.4 4.1 %fusion.18 = f32[2,12,96,128]{3,2,1,0:T(8,128)S(1)} fusion(f32[2,12,96,128]{3,2,1,0:T(8,128)S(1)} %multiply_subtract_fusion.4, f32[2,12,1,128]{3,2,1,0:T(1,128)} %get-tuple-element.73, f32[2,12,95,128]{3,2,1,0:T(8,128)S(1)} %copy-done.35, f32[2,12,1,128]{3,2,1,0:T(1,128)S(1)} %get-tuple-element.72, f32[2,12,96,128]{3,2,1,0:T(8,128)S(1)} %get-tuple-element.22, ...), kind=kLoop, calls=%fused_computation.47 | loop fusion | flops 7962624 | bytes 12429760 | tf_op jit(solution)/shard_map/min | solution.py:107
  122.5 3.0 %fusion.1 = (f32[4,12,96,1]{3,2,1,0:T(8,128)}, f32[4,12,96,1]{3,2,1,0:T(8,128)}) fusion(f32[2,12,96,128]{3,2,1,0:T(8,128)S(1)} %get-tuple-element.18, f32[2,12,96,128]{3,2,1,0:T(8,128)S(1)} %fusion.18), kind=kLoop, calls=%fused_computation.24 | loop fusion | flops 9216 | bytes 2396160 | tf_op jit(solution)/shard_map/concatenate | solution.py:108
  125.5 3.0 %fusion.2 = (f32[4,12,96,127]{3,2,1,0:T(8,128)}, f32[4,12,96,127]{3,2,1,0:T(8,128)}) fusion(f32[2,12,96,128]{3,2,1,0:T(8,128)S(1)} %get-tuple-element.18, f32[2,12,96,128]{3,2,1,0:T(8,128)S(1)} %fusion.18), kind=kLoop, calls=%fused_computation.25 | loop fusion | flops 1170432 | bytes 7041024 | tf_op jit(solution)/shard_map/concatenate | solution.py:108
  132.2 4.9 %collective-permute-start.11 = (f32[4,12,1,128]{3,2,1,0:T(1,128)}, f32[4,12,1,128]{3,2,1,0:T(1,128)}, u32[]{:S(2)}, u32[]{:S(2)}) collective-permute-start(f32[4,12,1,128]{3,2,1,0:T(1,128)} %get-tuple-element.52), channel_id=1, source_target_pairs={{0,1},{1,2},{2,3},{4,5},{5,6},{6,7},{8,9},{9,10},{10,11},{12,13},{... | collective-permute-start | bytes 73736 | tf_op jit(solution)/shard_map/ppermute | solution.py:25
  137.0 3.0 %copy.968 = f32[4,12,96,1]{2,0,3,1:T(4,128)} copy(f32[4,12,96,1]{3,2,1,0:T(8,128)} %get-tuple-element.49) | data formatting | bytes 36864 | tf_op jit(solution)/shard_map/slice | solution.py:223
  140.7 3.0 %copy.970 = f32[4,12,96,1]{2,0,3,1:T(4,128)} copy(f32[4,12,96,1]{3,2,1,0:T(8,128)} %get-tuple-element.50) | data formatting | bytes 36864 | tf_op jit(solution)/shard_map/slice | solution.py:223
  143.7 10.3 %all_gather.14 = f32[4,12,1,1024]{3,0,2,1:T(4,128)} all-gather(f32[4,12,1,128]{3,0,2,1:T(4,128)} %copy.972), channel_id=1, replica_groups=mesh['lon'=8,'lat'=4] {'lon'}, dimensions={3}, use_global_device_ids=true | all-gather | bytes 221184 | tf_op jit(solution)/shard_map/all_gather | solution.py:233
  154.1 2.6 %copy.973 = f32[4,12,1,1024]{1,0,3,2:T(4,128)} copy(f32[4,12,1,1024]{3,0,2,1:T(4,128)} %all_gather.14) | data formatting | bytes 393216 | tf_op jit(solution)/shard_map/all_gather | solution.py:233
  156.7 3.2 %gather_fusion.2 = f32[128,4,12]{2,1,0:T(4,128)} fusion(f32[4,12,1024]{1,0,2:T(4,128)} %bitcast.133, s32[1024]{0:T(1024)} %pad_clamp_fusion.1), kind=kCustom, calls=%fused_computation.4 | custom fusion | bytes 49664 | tf_op jit(solution)/shard_map/jit(_take)/gather | solution.py:234
  164.3 3.2 %maximum_select_fusion.4 = f32[4,12,96,128]{3,2,1,0:T(8,128)S(1)} fusion(f32[4,12,96,1]{3,2,1,0:T(8,128)} %get-tuple-element.49, f32[4,12,96,127]{3,2,1,0:T(8,128)} %get-tuple-element.47, f32[4,12,96]{2,1,0:T(8,128)S(1)} %copy.969, pred[128]{0:T(512)(128)(4,1)S(1)} %copy-done.89), kind=kLoop, calls=%fused_computation.31 | loop fusion | flops 1179648 | bytes 4737152 | tf_op jit(solution)/shard_map/jit(_where)/select_n | solution.py:43
  174.4 2.1 fusion.23
  181.6 5.1 %collective-permute-start.15 = (f32[2,12,1,128]{3,2,1,0:T(1,128)S(1)}, f32[2,12,1,128]{3,2,1,0:T(1,128)}, u32[]{:S(2)}, u32[]{:S(2)}) collective-permute-start(f32[2,12,1,128]{3,2,1,0:T(1,128)S(1)} %get-tuple-element.65), channel_id=1, source_target_pairs={{0,1},{1,2},{2,3},{4,5},{5,6},{6,7},{8,9},{9,10},{10,11},{12,13},{... | collective-permute-start | bytes 36872 | tf_op jit(solution)/shard_map/ppermute | solution.py:25
  188.6 2.2 fusion.39
  191.8 10.2 %all_gather.15 = f32[2,12,1,1024]{3,0,2,1:T(2,128)} all-gather(f32[2,12,1,128]{3,0,2,1:T(2,128)} %copy.984), channel_id=1, replica_groups=mesh['lon'=8,'lat'=4] {'lon'}, dimensions={3}, use_global_device_ids=true | all-gather | bytes 110592 | tf_op jit(solution)/shard_map/all_gather | solution.py:233
  202.0 2.1 copy.985
  204.1 2.8 %gather_fusion.4 = f32[128,2,12]{2,1,0:T(2,128)} fusion(f32[2,12,1024]{1,0,2:T(2,128)} %copy.985, s32[1024]{0:T(1024)} %pad_clamp_fusion), kind=kCustom, calls=%fused_computation.1.clone | custom fusion | bytes 25088 | tf_op jit(solution)/shard_map/jit(_take)/gather | solution.py:234
  223.9 3.0 %multiply_add_fusion = f32[2,12,96,128]{3,2,1,0:T(8,128)S(1)} fusion(f32[2,12,96,128]{3,2,1,0:T(8,128)S(1)} %fusion.23, f32[2,11,96,128]{3,2,1,0:T(8,128)S(1)} %fusion.35, f32[2,11,96,128]{3,2,1,0:T(8,128)S(1)} %fusion.36, f32[2,11,96,128]{3,2,1,0:T(8,128)S(1)} %fusion.37, f32[2,11,96,128]{3,2,1,0:T(8,128)S(1)} %fusion.38, ...), kind=kLoop, calls=%fused_computation.81 | loop fusion | flops 9732096 | bytes 17836480 | tf_op jit(solution)/shard_map/add | solution.py:176
  (311 shorter events, 86.1 us)
Async XLA Ops:
  0.6 22.7 %copy-start = (s32[1024]{0:T(1024)S(1)}, s32[1024]{0:T(1024)}, u32[]{:S(2)}) copy-start(s32[1024]{0:T(1024)} %param.19) | copy-start | bytes 12292
  4.6 61.2 %collective-permute-start.2 = (f32[5,12,1,128]{3,2,1,0:T(1,128)}, f32[5,12,1,128]{3,2,1,0:T(1,128)}, u32[]{:S(2)}, u32[]{:S(2)}) collective-permute-start(f32[5,12,1,128]{3,2,1,0:T(1,128)} %get-tuple-element.45), channel_id=1, source_target_pairs={{1,0},{2,1},{3,2},{5,4},{6,5},{7,6},{9,8},{10,9},{11,10},{13,12},{... | collective-permute-start | bytes 92168 | tf_op jit(solution)/shard_map/ppermute | solution.py:27
  5.9 63.7 %collective-permute-start.3 = (f32[5,12,1,128]{3,2,1,0:T(1,128)}, f32[5,12,1,128]{3,2,1,0:T(1,128)}, u32[]{:S(2)}, u32[]{:S(2)}) collective-permute-start(f32[5,12,1,128]{3,2,1,0:T(1,128)} %get-tuple-element.46), channel_id=1, source_target_pairs={{0,1},{1,2},{2,3},{4,5},{5,6},{6,7},{8,9},{9,10},{10,11},{12,13},{... | collective-permute-start | bytes 92168 | tf_op jit(solution)/shard_map/ppermute | solution.py:25
  18.6 37.0 %collective-permute-start = (f32[5,12,96,1]{2,3,1,0:T(1,128)}, f32[5,12,96,1]{2,3,1,0:T(1,128)}, u32[]{:S(2)}, u32[]{:S(2)}) collective-permute-start(f32[5,12,96,1]{2,3,1,0:T(1,128)} %copy.952), channel_id=1, source_target_pairs={{4,0},{8,4},{12,8},{16,12},{20,16},{24,20},{28,24},{0,28},{5,1},{9... | collective-permute-start | bytes 69128 | tf_op jit(solution)/shard_map/ppermute | solution.py:27
  23.3 38.2 %collective-permute-start.1 = (f32[5,12,96,1]{2,3,1,0:T(1,128)}, f32[5,12,96,1]{2,3,1,0:T(1,128)}, u32[]{:S(2)}, u32[]{:S(2)}) collective-permute-start(f32[5,12,96,1]{2,3,1,0:T(1,128)} %copy.953), channel_id=1, source_target_pairs={{0,4},{4,8},{8,12},{12,16},{16,20},{20,24},{24,28},{28,0},{1,5},{5... | collective-permute-start | bytes 69128 | tf_op jit(solution)/shard_map/ppermute | solution.py:25
  28.5 190.9 %copy-start.78 = (pred[96]{0:T(512)(128)(4,1)}, pred[96]{0:T(512)(128)(4,1)S(1)}, u32[]{:S(2)}) copy-start(pred[96]{0:T(512)(128)(4,1)S(1)} %get-tuple-element.95) | copy-start | bytes 292
  32.9 43.1 %copy-start.11 = (f32[12,96,128]{2,1,0:T(8,128)}, f32[12,96,128]{2,1,0:T(8,128)S(1)}, u32[]{:S(2)}) copy-start(f32[12,96,128]{2,1,0:T(8,128)S(1)} %fusion.83) | copy-start | bytes 1769476
  59.6 16.4 %copy-start.8 = (f32[5,12,96,128]{3,2,1,0:T(8,128)}, f32[5,12,96,128]{3,2,1,0:T(8,128)S(1)}, u32[]{:S(2)}) copy-start(f32[5,12,96,128]{3,2,1,0:T(8,128)S(1)} %maximum_select_fusion) | copy-start | bytes 8847364
  64.0 12.0 %copy-start.9 = (f32[5,12,96,128]{3,2,1,0:T(8,128)}, f32[5,12,96,128]{3,2,1,0:T(8,128)S(1)}, u32[]{:S(2)}) copy-start(f32[5,12,96,128]{3,2,1,0:T(8,128)S(1)} %maximum_select_fusion.1) | copy-start | bytes 8847364
  68.2 20.3 %copy-start.6 = (f32[5,12,96,128]{3,2,1,0:T(8,128)}, f32[5,12,96,128]{3,2,1,0:T(8,128)S(1)}, u32[]{:S(2)}) copy-start(f32[5,12,96,128]{3,2,1,0:T(8,128)S(1)} %maximum_select_fusion.2) | copy-start | bytes 8847364
  73.7 15.7 %copy-start.7 = (f32[5,12,96,128]{3,2,1,0:T(8,128)}, f32[5,12,96,128]{3,2,1,0:T(8,128)S(1)}, u32[]{:S(2)}) copy-start(f32[5,12,96,128]{3,2,1,0:T(8,128)S(1)} %maximum_select_fusion.3) | copy-start | bytes 8847364
  79.2 13.9 %copy-start.15 = (f32[2,12,96,1]{3,2,1,0:T(8,128)}, f32[2,12,96,1]{3,2,1,0:T(8,128)S(1)}, u32[]{:S(2)}) copy-start(f32[2,12,96,1]{3,2,1,0:T(8,128)S(1)} %get-tuple-element.69) | copy-start | bytes 27652
  79.2 28.6 %copy-start.14 = (f32[2,12,96,1]{3,2,1,0:T(8,128)}, f32[2,12,96,1]{3,2,1,0:T(8,128)S(1)}, u32[]{:S(2)}) copy-start(f32[2,12,96,1]{3,2,1,0:T(8,128)S(1)} %get-tuple-element.68) | copy-start | bytes 27652
  83.6 23.5 %collective-permute-start.7 = (f32[2,12,1,128]{3,2,1,0:T(1,128)S(1)}, f32[2,12,1,128]{3,2,1,0:T(1,128)}, u32[]{:S(2)}, u32[]{:S(2)}) collective-permute-start(f32[2,12,1,128]{3,2,1,0:T(1,128)S(1)} %get-tuple-element.72), channel_id=1, source_target_pairs={{0,1},{1,2},{2,3},{4,5},{5,6},{6,7},{8,9},{9,10},{10,11},{12,13},{... | collective-permute-start | bytes 36872 | tf_op jit(solution)/shard_map/ppermute | solution.py:25
  90.2 16.1 %collective-permute-start.6 = (f32[2,12,1,128]{3,2,1,0:T(1,128)}, f32[2,12,1,128]{3,2,1,0:T(1,128)}, u32[]{:S(2)}, u32[]{:S(2)}) collective-permute-start(f32[2,12,1,128]{3,2,1,0:T(1,128)} %get-tuple-element.73), channel_id=1, source_target_pairs={{1,0},{2,1},{3,2},{5,4},{6,5},{7,6},{9,8},{10,9},{11,10},{13,12},{... | collective-permute-start | bytes 36872 | tf_op jit(solution)/shard_map/ppermute | solution.py:27
  92.5 12.4 %collective-permute-start.4 = (f32[2,12,96,1]{2,0,3,1:T(2,128)}, f32[2,12,96,1]{2,0,3,1:T(2,128)}, u32[]{:S(2)}, u32[]{:S(2)}) collective-permute-start(f32[2,12,96,1]{2,0,3,1:T(2,128)} %copy.956), channel_id=1, source_target_pairs={{4,0},{8,4},{12,8},{16,12},{20,16},{24,20},{28,24},{0,28},{5,1},{9... | collective-permute-start | bytes 27656 | tf_op jit(solution)/shard_map/ppermute | solution.py:27
  94.0 11.5 %collective-permute-start.5 = (f32[2,12,96,1]{2,0,3,1:T(2,128)}, f32[2,12,96,1]{2,0,3,1:T(2,128)}, u32[]{:S(2)}, u32[]{:S(2)}) collective-permute-start(f32[2,12,96,1]{2,0,3,1:T(2,128)} %copy.958), channel_id=1, source_target_pairs={{0,4},{4,8},{8,12},{12,16},{16,20},{20,24},{24,28},{28,0},{1,5},{5... | collective-permute-start | bytes 27656 | tf_op jit(solution)/shard_map/ppermute | solution.py:25
  107.8 10.4 %copy-start.16 = (f32[2,12,96,1]{3,2,1,0:T(8,128)S(1)}, f32[2,12,96,1]{3,2,1,0:T(8,128)}, u32[]{:S(2)}) copy-start(f32[2,12,96,1]{3,2,1,0:T(8,128)} %copy-done.15) | copy-start | bytes 27652
  107.8 10.4 %copy-start.32 = (f32[2,12,96,127]{3,2,1,0:T(8,128)S(1)}, f32[2,12,96,127]{3,2,1,0:T(8,128)}, u32[]{:S(2)}) copy-start(f32[2,12,96,127]{3,2,1,0:T(8,128)} %get-tuple-element.66) | copy-start | bytes 3511300
  107.8 10.4 %copy-start.33 = (f32[2,12,96,127]{3,2,1,0:T(8,128)S(1)}, f32[2,12,96,127]{3,2,1,0:T(8,128)}, u32[]{:S(2)}) copy-start(f32[2,12,96,127]{3,2,1,0:T(8,128)} %get-tuple-element.67) | copy-start | bytes 3511300
  107.8 10.4 %copy-start.34 = (f32[2,12,95,128]{3,2,1,0:T(8,128)S(1)}, f32[2,12,95,128]{3,2,1,0:T(8,128)}, u32[]{:S(2)}) copy-start(f32[2,12,95,128]{3,2,1,0:T(8,128)} %get-tuple-element.70) | copy-start | bytes 3502084
  107.8 10.4 %copy-start.35 = (f32[2,12,95,128]{3,2,1,0:T(8,128)S(1)}, f32[2,12,95,128]{3,2,1,0:T(8,128)}, u32[]{:S(2)}) copy-start(f32[2,12,95,128]{3,2,1,0:T(8,128)} %get-tuple-element.71) | copy-start | bytes 3502084
  107.8 10.4 %copy-start.66 = (pred[12,96,128]{2,1,0:T(8,128)(4,1)S(1)}, pred[12,96,128]{2,1,0:T(8,128)(4,1)}, u32[]{:S(2)}) copy-start(pred[12,96,128]{2,1,0:T(8,128)(4,1)} %bitcast_compare_fusion.1) | copy-start | bytes 442372
  122.5 47.9 %copy-start.2 = (f32[2,12,96,128]{3,2,1,0:T(8,128)}, f32[2,12,96,128]{3,2,1,0:T(8,128)S(1)}, u32[]{:S(2)}) copy-start(f32[2,12,96,128]{3,2,1,0:T(8,128)S(1)} %fusion.18) | copy-start | bytes 3538948
  132.2 37.4 %collective-permute-start.11 = (f32[4,12,1,128]{3,2,1,0:T(1,128)}, f32[4,12,1,128]{3,2,1,0:T(1,128)}, u32[]{:S(2)}, u32[]{:S(2)}) collective-permute-start(f32[4,12,1,128]{3,2,1,0:T(1,128)} %get-tuple-element.52), channel_id=1, source_target_pairs={{0,1},{1,2},{2,3},{4,5},{5,6},{6,7},{8,9},{9,10},{10,11},{12,13},{... | collective-permute-start | bytes 73736 | tf_op jit(solution)/shard_map/ppermute | solution.py:25
  140.0 22.8 %collective-permute-start.8 = (f32[4,12,96,1]{2,0,3,1:T(4,128)}, f32[4,12,96,1]{2,0,3,1:T(4,128)}, u32[]{:S(2)}, u32[]{:S(2)}) collective-permute-start(f32[4,12,96,1]{2,0,3,1:T(4,128)} %copy.968), channel_id=1, source_target_pairs={{4,0},{8,4},{12,8},{16,12},{20,16},{24,20},{28,24},{0,28},{5,1},{9... | collective-permute-start | bytes 55304 | tf_op jit(solution)/shard_map/ppermute | solution.py:27
  143.7 19.8 %collective-permute-start.9 = (f32[4,12,96,1]{2,0,3,1:T(4,128)}, f32[4,12,96,1]{2,0,3,1:T(4,128)}, u32[]{:S(2)}, u32[]{:S(2)}) collective-permute-start(f32[4,12,96,1]{2,0,3,1:T(4,128)} %copy.970), channel_id=1, source_target_pairs={{0,4},{4,8},{8,12},{12,16},{16,20},{20,24},{24,28},{28,0},{1,5},{5... | collective-permute-start | bytes 55304 | tf_op jit(solution)/shard_map/ppermute | solution.py:25
  161.5 8.0 %collective-permute-start.10 = (f32[4,12,1,128]{3,2,1,0:T(1,128)}, f32[4,12,1,128]{3,2,1,0:T(1,128)S(1)}, u32[]{:S(2)}, u32[]{:S(2)}) collective-permute-start(f32[4,12,1,128]{3,2,1,0:T(1,128)} %get-tuple-element.51), channel_id=1, source_target_pairs={{1,0},{2,1},{3,2},{5,4},{6,5},{7,6},{9,8},{10,9},{11,10},{13,12},{... | collective-permute-start | bytes 73736 | tf_op jit(solution)/shard_map/ppermute | solution.py:27
  181.6 35.9 %collective-permute-start.15 = (f32[2,12,1,128]{3,2,1,0:T(1,128)S(1)}, f32[2,12,1,128]{3,2,1,0:T(1,128)}, u32[]{:S(2)}, u32[]{:S(2)}) collective-permute-start(f32[2,12,1,128]{3,2,1,0:T(1,128)S(1)} %get-tuple-element.65), channel_id=1, source_target_pairs={{0,1},{1,2},{2,3},{4,5},{5,6},{6,7},{8,9},{9,10},{10,11},{12,13},{... | collective-permute-start | bytes 36872 | tf_op jit(solution)/shard_map/ppermute | solution.py:25
  187.7 22.0 %collective-permute-start.12 = (f32[2,12,96,1]{2,0,3,1:T(2,128)}, f32[2,12,96,1]{2,0,3,1:T(2,128)}, u32[]{:S(2)}, u32[]{:S(2)}) collective-permute-start(f32[2,12,96,1]{2,0,3,1:T(2,128)} %copy.980), channel_id=1, source_target_pairs={{4,0},{8,4},{12,8},{16,12},{20,16},{24,20},{28,24},{0,28},{5,1},{9... | collective-permute-start | bytes 27656 | tf_op jit(solution)/shard_map/ppermute | solution.py:27
  191.8 18.7 %collective-permute-start.13 = (f32[2,12,96,1]{2,0,3,1:T(2,128)}, f32[2,12,96,1]{2,0,3,1:T(2,128)}, u32[]{:S(2)}, u32[]{:S(2)}) collective-permute-start(f32[2,12,96,1]{2,0,3,1:T(2,128)} %copy.982), channel_id=1, source_target_pairs={{0,4},{4,8},{8,12},{12,16},{16,20},{20,24},{24,28},{28,0},{1,5},{5... | collective-permute-start | bytes 27656 | tf_op jit(solution)/shard_map/ppermute | solution.py:25
  208.4 8.9 %collective-permute-start.14 = (f32[2,12,1,128]{3,2,1,0:T(1,128)}, f32[2,12,1,128]{3,2,1,0:T(1,128)S(1)}, u32[]{:S(2)}, u32[]{:S(2)}) collective-permute-start(f32[2,12,1,128]{3,2,1,0:T(1,128)} %get-tuple-element.64), channel_id=1, source_target_pairs={{1,0},{2,1},{3,2},{5,4},{6,5},{7,6},{9,8},{10,9},{11,10},{13,12},{... | collective-permute-start | bytes 36872 | tf_op jit(solution)/shard_map/ppermute | solution.py:27
  (79 other events, 254.7 us)
where the time goes:
time: 231 us; the launch traced here: 228 us
  local copies, waits for them, and re-layouts  88.2 us (38%)
  other arithmetic  67.9 us (29%)
  blocking collectives  41.2 us (18%)
  starting transfers between devices  28.7 us (12%)
    all_gather x4, blocking collectives, device_sides(): top_row = lax.all_gather(stack[:, :, -1:, :], 'lon', axis=3, tiled=True)  41.2 us
    slice x11, local copies, waits for them, and re-layouts, rim_sides(): columns = jnp.concatenate([stack[..., :1], stack[..., -1:]], axis=3)  20.1 us
    ppermute x8, starting transfers between devices, extended(): lax.ppermute(tail, axis, [(i, (i + 1) % count) for i in range(ends)])  19.6 us
    unnamed x198, local copies, waits for them, and re-layouts  16.3 us
    gather x8, local copies, waits for them, and re-layouts, device_sides(): fold_row = jnp.take(top_row, facing, axis=3) * signs  15.7 us
    min x1, other arithmetic, ratios(): jnp.minimum(1.0, (highest - value_centre) / jnp.maximum(inflow, RATIO_FLO...  10.3 us
    ppermute x8, starting transfers between devices, extended(): lax.ppermute(head, axis, [((i + 1) % count, i) for i in range(ends)])  9.02 us
    select_n x3, other arithmetic, sided(): jnp.where(lane == width - 1, east_col, jnp.roll(core, -1, axis=-1))  8.44 us
  transfers between devices with their start and end apart: 16, of which 0 were waited for; matrix products, arithmetic and copies ran while one was open for 39% of the time, Pallas kernels for 0%

commit v1 on v0

v1 whole, which is shorter than its diff:
```python
import functools

import jax
import jax.numpy as jnp
from jax import lax
from jax.experimental import pallas as pl
from jax.experimental.pallas import tpu as pltpu
from jax.sharding import PartitionSpec as P

RATIO_FLOOR = 0.05
DIFFUSIVITY = 0.1
THERMAL_COEF = 0.2
HALINE_COEF = 0.8

HALO = 4
SUB = 8
LANES = 128
VMEM_BYTES = 56 * 1024 * 1024


def sublanes():
    return lax.broadcasted_iota(jnp.int32, (SUB, LANES), 0)


def lanes():
    return lax.broadcasted_iota(jnp.int32, (SUB, LANES), 1)


def half_turn(tile):
    return pltpu.roll(tile, 4, 0)


def as_mask(flag):
    return (jnp.zeros((SUB, LANES), jnp.int32) + flag) > 0


def wet_count(indicator, total):
    return jnp.where(indicator == 1, total, 0).astype(jnp.float32)


def pack_rows(levels, *refs):
    south, north, (ind_s, ind_n, tot_s, tot_n), (first, second) = refs[:4], refs[4:8], refs[8:12], refs[12:]
    lat = lax.axis_index("lat")
    odd = as_mask(lat % 2)
    upper = sublanes() >= HALO
    for i in range(2 * levels):
        f, k = divmod(i, levels)
        low = jnp.where(upper, half_turn(south[f + 2][k]), south[f][k])
        high = jnp.where(upper, north[f][k], half_turn(north[f + 2][k]))
        first[i] = jnp.where(odd, low, high)
        second[i] = jnp.where(odd, high, low)
    low = wet_count(ind_s[...], tot_s[...])
    high = wet_count(ind_n[...], tot_n[...])
    first[2 * levels] = jnp.where(odd, low, high)
    second[2 * levels] = jnp.where(odd, high, low)

    @pl.when(lat == lax.axis_size("lat") - 1)
    def _():
        for i in range(2 * levels):
            f, k = divmod(i, levels)
            for j in range(HALO):
                second[i, j : j + 1, :] = north[f][k, 7 - j : 8 - j, :]
                row = 7 - j if f == 0 else (6, 5, 4, 7)[j]
                second[i, HALO + j : HALO + j + 1, :] = -north[f + 2][k, row : row + 1, :]
        for j in range(HALO):
            second[2 * levels, j : j + 1, :] = wet_count(ind_n[7 - j : 8 - j, :], tot_n[7 - j : 8 - j, :])


def pack_columns(levels, tiles, *refs):
    fields, ind, tot, q1, q2, own, to_east, to_west = refs[:4], *refs[4:]
    odd = as_mask(lax.axis_index("lat") % 2)
    lane = lanes()
    upper = sublanes() >= HALO
    count = 4 * levels + 1
    half = 2 * levels

    def halo_tile(fl):
        i = fl % half
        one, two = q1[2 * levels if fl == 2 * half else i], q2[2 * levels if fl == 2 * half else i]
        north, south = jnp.where(odd, two, one), jnp.where(odd, one, two)
        if half <= fl < 2 * half:
            return half_turn(jnp.where(upper, north, south))
        return jnp.where(upper, south, north)

    def piece(fl, t):
        if t >= tiles:
            return halo_tile(fl)
        rows = pl.ds(t * SUB, SUB)
        if fl == 2 * half:
            return wet_count(ind[rows, :], tot[rows, :])
        f, k = divmod(fl, levels)
        return fields[f][k, rows, :]

    for g in range(0, count, 8):
        members = range(g, min(g + 8, count))
        column = []
        for t in range(tiles + 1):
            tile = None
            for j, fl in enumerate(members):
                moved = pltpu.roll(piece(fl, t), (16 * j + 8) % LANES, 1)
                tile = moved if tile is None else jnp.where(lane >= 16 * j, moved, tile)
            column.append(tile)
        while len(column) < LANES // SUB:
            column.append(column[tiles])
        turned = jnp.concatenate(column, axis=0).T
        for j, fl in enumerate(members):
            own[fl] = turned[16 * j : 16 * j + 16]
    for i in range(half):
        to_east[i] = jnp.where(upper, own[i, 0:8, :], half_turn(own[i + half, 0:8, :]))
        to_west[i] = jnp.where(upper, half_turn(own[i + half, 8:16, :]), own[i, 8:16, :])
    to_east[half] = own[2 * half, 0:8, :]
    to_west[half] = own[2 * half, 8:16, :]
    for i in range(half + 1):
        to_east[half + 1 + i] = q2[i]
        to_west[half + 1 + i] = q2[i]


def ahead(tiles):
    return tiles[1:] + [pltpu.roll(tiles[0], SUB - 1, 0)]


def behind(tiles):
    return [pltpu.roll(tiles[-1], 1, 0)] + tiles[:-1]


def right(tiles):
    return [pltpu.roll(x, LANES - 1, 1) for x in tiles]


def left(tiles):
    return [pltpu.roll(x, 1, 1) for x in tiles]


def each(function, *lists):
    return [function(*items) for items in zip(*lists)]


def replaced(tiles, other):
    return [other.get(t, x) for t, x in enumerate(tiles)]


def flux_pair(q, q_next, half_speed, half_size):
    anti = half_size * (q_next - q)
    return half_speed * (q_next + q) - anti, anti


def limited_flux(anti, plus, minus, plus_next, minus_next):
    return anti * jnp.where(anti >= 0.0, jnp.minimum(plus_next, minus), jnp.minimum(plus, minus_next))


def reciprocal(x):
    return pl.reciprocal(x, approx=True)


def advect(tracer, along, across, open_along, open_across, along_alt, across_alt):
    q_a, q_c = ahead(tracer), right(tracer)
    low_a, anti_a = map(list, zip(*each(flux_pair, tracer, q_a, *along)))
    low_c, anti_c = map(list, zip(*each(flux_pair, tracer, q_c, *across)))
    alt_a = {t: flux_pair(tracer[t], q_a[t], *v) for t, v in along_alt.items()}
    alt_c = {t: flux_pair(tracer[t], q_c[t], *v) for t, v in across_alt.items()}
    low_b = behind(replaced(low_a, {t: v[0] for t, v in alt_a.items()}))
    anti_b = behind(replaced(anti_a, {t: v[1] for t, v in alt_a.items()}))
    low_l = left(replaced(low_c, {t: v[0] for t, v in alt_c.items()}))
    anti_l = left(replaced(anti_c, {t: v[1] for t, v in alt_c.items()}))
    upwind = each(lambda q, a, b, c, d: q - ((a - b) + (c - d)), tracer, low_a, low_b, low_c, low_l)

    up_a, up_c = ahead(upwind), right(upwind)
    step_a = each(lambda u, n, m: jnp.where(m, n - u, 0.0), upwind, up_a, open_along)
    step_c = each(lambda u, n, m: jnp.where(m, n - u, 0.0), upwind, up_c, open_across)
    step_b, step_l = behind(step_a), left(step_c)

    def ratios(a, b, c, l, sa, sb, sc, sl):
        inflow = (jnp.maximum(b, 0.0) - jnp.minimum(a, 0.0)) + (jnp.maximum(l, 0.0) - jnp.minimum(c, 0.0))
        outflow = (jnp.maximum(a, 0.0) - jnp.minimum(b, 0.0)) + (jnp.maximum(c, 0.0) - jnp.minimum(l, 0.0))
        rise = jnp.maximum(jnp.maximum(jnp.maximum(sa, sc), 0.0), -jnp.minimum(sb, sl))
        drop = jnp.maximum(jnp.maximum(jnp.maximum(sb, sl), 0.0), -jnp.minimum(sa, sc))
        plus = jnp.minimum(1.0, rise * reciprocal(jnp.maximum(inflow, RATIO_FLOOR)))
        minus = jnp.minimum(1.0, drop * reciprocal(jnp.maximum(outflow, RATIO_FLOOR)))
        return plus, minus

    plus, minus = map(
        list, zip(*each(ratios, anti_a, anti_b, anti_c, anti_l, step_a, step_b, step_c, step_l))
    )
    plus_a, minus_a, plus_c, minus_c = ahead(plus), ahead(minus), right(plus), right(minus)
    lim_a = each(limited_flux, anti_a, plus, minus, plus_a, minus_a)
    lim_c = each(limited_flux, anti_c, plus, minus, plus_c, minus_c)
    lim_b = behind(
        replaced(lim_a, {t: limited_flux(v[1], plus[t], minus[t], plus_a[t], minus_a[t]) for t, v in alt_a.items()})
    )
    lim_l = left(
        replaced(lim_c, {t: limited_flux(v[1], plus[t], minus[t], plus_c[t], minus_c[t]) for t, v in alt_c.items()})
    )
    return each(lambda u, a, b, c, d: u - ((a - b) + (c - d)), upwind, lim_a, lim_b, lim_c, lim_l)


def diffuse(temp, salt, temp_below, salt_below, stacked, open_along, open_across):
    dz_t = each(lambda x, y, m: jnp.where(m, y - x, 0.0), temp, temp_below, stacked)
    dz_s = each(lambda x, y, m: jnp.where(m, y - x, 0.0), salt, salt_below, stacked)

    def face(t0, t1, s0, s1, zt0, zt1, zs0, zs1, m):
        dt, ds, zt, zs = t1 - t0, s1 - s0, zt1 + zt0, zs1 + zs0
        bottom = jnp.maximum(HALINE_COEF * zs - THERMAL_COEF * zt, 1.0)
        half_slope = (HALINE_COEF * ds - THERMAL_COEF * dt) * reciprocal(bottom)
        half_slope = jnp.maximum(jnp.minimum(half_slope, 1.0), -1.0)
        return jnp.where(m, dt - half_slope * zt, 0.0), jnp.where(m, ds - half_slope * zs, 0.0)

    def faces(shift, mask):
        parts = each(face, temp, shift(temp), salt, shift(salt), dz_t, shift(dz_t), dz_s, shift(dz_s), mask)
        return map(list, zip(*parts))

    t_a, s_a = faces(ahead, open_along)
    t_c, s_c = faces(right, open_across)

    def total(q, a, b, c, d):
        return q + DIFFUSIVITY * ((a - b) + (c - d))

    return (
        each(total, temp, t_a, behind(t_a), t_c, left(t_c)),
        each(total, salt, s_a, behind(s_a), s_c, left(s_c)),
    )


def halves(speed, mask):
    half = jnp.where(mask, 0.5 * speed, 0.0)
    return half, jnp.abs(half)


def step(levels, rows, *refs):
    (
        seam, q1, q2, from_east, from_west, own, ind, tot, temp_in, salt_in, east_in, north_in,
        temp_out, salt_out,
        pad, count, opens, strip, strip_opens, north_halo, adv, strip_adv, out, strip_out, sems,
    ) = refs
    half = 2 * levels
    flat = 4 * levels
    nt = rows // SUB + 1
    period = nt * SUB
    width = LANES
    nl = lax.axis_size("lon")
    lat = lax.axis_index("lat")
    on_top = lat == lax.axis_size("lat") - 1
    odd = as_mask(lat % 2)
    lane, sub = lanes(), sublanes()
    upper = sub >= HALO
    tops = as_mask(on_top.astype(jnp.int32))

    loads = [
        pltpu.make_async_copy(ref, pad.at[f, :, 0:rows, :], sems.at[f])
        for f, ref in enumerate((temp_in, salt_in, east_in, north_in))
    ]
    for load in loads:
        load.start()

    for i in range(half + 1):
        north_halo[i] = jnp.where(odd, q2[i], q1[i])
        if i < half:
            strip[i, 8:16, :] = jnp.where(upper, from_west[i], from_east[i])
            strip[i + half, 8:16, :] = half_turn(jnp.where(upper, from_east[i], from_west[i]))
        else:
            strip[flat, 8:16, :] = jnp.where(upper, from_west[i], from_east[i])
    for fl in range(flat + 1):
        strip[fl, 0:8, :] = own[fl, 0:8, :]
        strip[fl, 16:24, :] = own[fl, 8:16, :]

    @pl.when(on_top)
    def _():
        r = seam[0] % width
        shift = r + jnp.where(2 * r < width, width, 0)

        def facing(i, column):
            at = shift - column - jnp.where(upper, 1 if i < levels else 0, 0)
            index = at & (width - 1)

            def pick(tile):
                return jnp.take_along_axis(tile, index, axis=1, mode="promise_in_bounds")

            here = pick(q2[i])
            east = pick(from_east[half + 1 + i])
            west = pick(from_west[half + 1 + i])
            return jnp.where(at < 0, east, jnp.where(at >= width, west, here))

        edge = jnp.where(lane < 12, 120 + lane, lane - 16)
        corner = []
        for i in range(half + 1):
            north_halo[i] = facing(i, lane)
            corner.append(facing(i, edge))
        while len(corner) % 16:
            corner.append(jnp.zeros((SUB, LANES), jnp.float32))
        here = (lane >= rows) & (lane < rows + HALO)
        for g in range(0, len(corner), 16):
            turned = jnp.concatenate(corner[g : g + 16], axis=0).T
            for i in range(g, min(g + 16, half + 1)):
                for fl, at in ((i, 0), (i + half, HALO)) if i < half else ((flat, 0),):
                    for a in range(0, 24, 8):
                        moved = pltpu.roll(turned[a : a + 8], (rows - 8 * (i - g) - at) % LANES, 1)
                        strip[fl, a : a + 8, :] = jnp.where(here, moved, strip[fl, a : a + 8, :])

    for i in range(half):
        f, k = divmod(i, levels)
        n_tile, s_tile = north_halo[i], jnp.where(odd, q1[i], q2[i])
        pad[f, k, rows:period, :] = jnp.where(upper, s_tile, n_tile)
        pad[f + 2, k, rows:period, :] = half_turn(jnp.where(upper, n_tile, s_tile))
    count[0:rows, :] = wet_count(ind[...], tot[...])
    count[rows:period, :] = jnp.where(upper, jnp.where(odd, q1[half], q2[half]), north_halo[half])

    def open_counts(source, target, tiles):
        n = [source[pl.ds(t, SUB, stride=tiles), :] for t in range(tiles)]
        for t, (c, a, b) in enumerate(zip(n, ahead(n), right(n))):
            target[0, t] = c
            target[1, t] = jnp.minimum(c, a)
            target[2, t] = jnp.minimum(c, b)

    open_counts(count, opens, nt)
    open_counts(strip.at[flat], strip_opens, 3)

    def wet_faces(source, tiles, k):
        level = k.astype(jnp.float32)
        return (
            [source[1, t] > level for t in range(tiles)],
            [source[2, t] > level for t in range(tiles)],
            [source[0, t] > level + 1.0 for t in range(tiles)],
        )

    for load in loads:
        load.wait()

    seam_tile = (rows - 1) % nt
    seam_sub = (rows - 1) // nt
    spare_tile = (rows + HALO - 1) % nt

    def main_advect(k, carry):
        def tiles_of(f):
            return [pad.at[f, k][pl.ds(t, SUB, stride=nt), :] for t in range(nt)]

        along_open, across_open, _ = wet_faces(opens, nt, k)
        v = tiles_of(3)
        along = list(zip(*each(halves, v, along_open)))
        across = list(zip(*each(halves, tiles_of(2), across_open)))
        turned = jnp.where((sub == seam_sub) & tops, v[spare_tile], v[seam_tile])
        alt = {seam_tile: halves(turned, along_open[seam_tile])}
        for f in range(2):
            result = advect(tiles_of(f), along, across, along_open, across_open, alt, {})
            for t in range(nt):
                adv[f, k, t] = result[t]
        return carry

    def strip_advect(group, carry):
        for j in range(4):
            k = group * 4 + j

            def tiles_of(f):
                return [strip.at[f * levels + k][pl.ds(t, SUB, stride=3), :] for t in range(3)]

            along_open, across_open, _ = wet_faces(strip_opens, 3, k)
            v = tiles_of(3)
            along = list(zip(*each(halves, tiles_of(2), along_open)))
            across = list(zip(*each(halves, v, across_open)))
            fold = (lane == rows - 1) & tops
            alt = {
                t: halves(jnp.where(fold, pltpu.roll(x, LANES - HALO, 1), x), m)
                for t, (x, m) in enumerate(zip(v, across_open))
            }
            for f in range(2):
                result = advect(tiles_of(f), along, across, along_open, across_open, {}, alt)
                for t in range(3):
                    strip_adv[f, k, t] = result[t]
        return carry

    def diffuse_level(source, counts, tiles, k):
        below = jnp.minimum(k + 1, levels - 1)
        along_open, across_open, stacked = wet_faces(counts, tiles, k)
        fields = [[source[f, at, t] for t in range(tiles)] for at in (k, below) for f in range(2)]
        return diffuse(*fields, stacked, along_open, across_open)

    def main_diffuse(k, carry):
        for f, result in enumerate(diffuse_level(adv, opens, nt, k)):
            for t in range(nt):
                out.at[f, k][pl.ds(t, SUB, stride=nt), :] = result[t]
        return carry

    def strip_diffuse(group, carry):
        for j in range(4):
            k = group * 4 + j
            for f, result in enumerate(diffuse_level(strip_adv, strip_opens, 3, k)):
                for t in range(3):
                    strip_out.at[f * levels + k][pl.ds(t, SUB, stride=3), :] = result[t]
        return carry

    lax.fori_loop(0, levels // 4, strip_advect, 0)
    lax.fori_loop(0, levels // 4, strip_diffuse, 0)
    lax.fori_loop(0, levels, main_advect, 0)
    lax.fori_loop(0, levels, main_diffuse, 0)

    at_edge = (lane < HALO) | (lane >= LANES - HALO)
    for g in range(0, half, 8):
        column = []
        for i in range(g, g + 8):
            column += [strip_out[i, 0:8, :], strip_out[i, 16:24, :]]
        turned = jnp.concatenate(column, axis=0).T
        for i in range(g, g + 8):
            f, k = divmod(i, levels)
            back = (LANES - 16 * (i - g) - 8) % LANES
            for t in range(rows // SUB):
                moved = pltpu.roll(turned[t * SUB : t * SUB + SUB], back, 1)
                at = pl.ds(t * SUB, SUB)
                out[f, k, at, :] = jnp.where(at_edge, moved, out[f, k, at, :])
    stores = [
        pltpu.make_async_copy(out.at[f, :, 0:rows, :], ref, sems.at[f])
        for f, ref in enumerate((temp_out, salt_out))
    ]
    for store in stores:
        store.start()
    for store in stores:
        store.wait()


def local(nl, nlat, temp, salt, east, north, indicator, total, seam):
    levels, rows, width = temp.shape
    half = 2 * levels
    vmem = pl.BlockSpec(memory_space=pltpu.VMEM)
    anywhere = pl.BlockSpec(memory_space=pl.ANY)
    params = pltpu.CompilerParams(vmem_limit_bytes=VMEM_BYTES)
    f32 = jnp.float32

    last = rows // SUB - 1
    low = pl.BlockSpec((levels, SUB, width), lambda i: (0, 0, 0))
    high = pl.BlockSpec((levels, SUB, width), lambda i: (0, last, 0))
    flat_low = pl.BlockSpec((SUB, width), lambda i: (0, 0))
    flat_high = pl.BlockSpec((SUB, width), lambda i: (last, 0))
    block = jax.ShapeDtypeStruct((half + 1, SUB, width), f32)
    whole_block = pl.BlockSpec((half + 1, SUB, width), lambda i: (0, 0, 0))
    fields = (temp, salt, east, north)
    first, second = pl.pallas_call(
        functools.partial(pack_rows, levels),
        grid=(1,),
        in_specs=[low] * 4 + [high] * 4 + [flat_low, flat_high] * 2,
        out_specs=[whole_block] * 2,
        out_shape=[block] * 2,
        compiler_params=params,
    )(*fields, *fields, indicator, indicator, total, total)

    pivot = seam[0]
    low_half = 2 * (pivot % width) < width
    turn = (pivot // width - low_half.astype(jnp.int32)) % nl
    q1 = lax.ppermute(first, "lat", [(j, j ^ 1) for j in range(nlat)])

    def meet(turned):
        pairs = [(i * nlat + j, i * nlat + (j + 1 if j % 2 else j - 1)) for i in range(nl) for j in range(1, nlat - 1)]
        pairs += [(i * nlat + nlat - 1, (turned - i) % nl * nlat + nlat - 1) for i in range(nl)]
        return lambda x: lax.ppermute(x, ("lon", "lat"), pairs)

    q2 = lax.switch(turn, [meet(t) for t in range(nl)], second)

    strip_count = 2 * half + 1
    payload = jax.ShapeDtypeStruct((2 * half + 2, SUB, width), f32)
    own, to_east, to_west = pl.pallas_call(
        functools.partial(pack_columns, levels, rows // SUB),
        in_specs=[vmem] * 8,
        out_specs=[vmem] * 3,
        out_shape=[jax.ShapeDtypeStruct((strip_count, 2 * SUB, width), f32), payload, payload],
        compiler_params=params,
    )(*fields, indicator, total, q1, q2)
    from_west = lax.ppermute(to_east, "lon", [(i, (i + 1) % nl) for i in range(nl)])
    from_east = lax.ppermute(to_west, "lon", [((i + 1) % nl, i) for i in range(nl)])

    nt = rows // SUB + 1
    period = nt * SUB
    return pl.pallas_call(
        functools.partial(step, levels, rows),
        in_specs=[pl.BlockSpec(memory_space=pltpu.SMEM)] + [vmem] * 7 + [anywhere] * 4,
        out_specs=[anywhere] * 2,
        out_shape=[jax.ShapeDtypeStruct(temp.shape, f32)] * 2,
        scratch_shapes=[
            pltpu.VMEM((4, levels, period, width), f32),
            pltpu.VMEM((period, width), f32),
            pltpu.VMEM((3, nt, SUB, width), f32),
            pltpu.VMEM((strip_count, 24, width), f32),
            pltpu.VMEM((3, 3, SUB, width), f32),
            pltpu.VMEM((half + 1, SUB, width), f32),
            pltpu.VMEM((2, levels, nt, SUB, width), f32),
            pltpu.VMEM((2, levels, 3, SUB, width), f32),
            pltpu.VMEM((2, levels, period, width), f32),
            pltpu.VMEM((half, 24, width), f32),
            pltpu.SemaphoreType.DMA((4,)),
        ],
        compiler_params=params,
    )(seam, q1, q2, from_east, from_west, own, indicator, total, *fields)


def solution(mesh):
    in_specs = (
        P(None, "lat", "lon"),
        P(None, "lat", "lon"),
        P(None, "lat", "lon"),
        P(None, "lat", "lon"),
        P("lat", "lon"),
        P("lat", "lon"),
        P(),
    )
    out_specs = (P(None, "lat", "lon"), P(None, "lat", "lon"))
    body = functools.partial(local, mesh.shape["lon"], mesh.shape["lat"])
    return jax.shard_map(body, mesh=mesh, in_specs=in_specs, out_specs=out_specs, check_vma=False)
```

time: 231 us -> 43.7 us (0.19)
  the two profiles are of different devices: /device:TPU:0 before, /device:TPU:16 now
where the time goes in v1:
time: 43.7 us; the launch traced here: 43.4 us
  Pallas kernels  20.7 us (47%)
  waiting for transfers between devices  12.8 us (29%)
  starting transfers between devices  4.09 us (9%)
  between operations  3.27 us (7%)
  local copies, waits for them, and re-layouts  2.51 us (6%)
    pallas_call x1, Pallas kernels, local(): pl.pallas_call(functools.partial(step, levels, rows), in_specs=[pl.BlockS...  15.5 us
    ppermute x1, waiting for transfers between devices, local(): lax.ppermute(to_west, 'lon', [((i + 1) % nl, i) for i in range(nl)])  5.34 us
    ppermute x1, waiting for transfers between devices, meet(): return lambda x: lax.ppermute(x, ('lon', 'lat'), pairs)  4.73 us
    pallas_call x1, Pallas kernels, local(): pl.pallas_call(functools.partial(pack_columns, levels, rows // SUB), in_s...  3.47 us
    ppermute x1, waiting for transfers between devices, local(): lax.ppermute(to_east, 'lon', [(i, (i + 1) % nl) for i in range(nl)])  2.73 us
    ppermute x1, starting transfers between devices, meet(): return lambda x: lax.ppermute(x, ('lon', 'lat'), pairs)  1.92 us
    pallas_call x1, Pallas kernels, local(): pl.pallas_call(functools.partial(pack_rows, levels), grid=(1,), in_specs=...  1.69 us
    ppermute x1, starting transfers between devices, local(): q1 = lax.ppermute(first, 'lat', [(j, j ^ 1) for j in range(nlat)])  1.66 us
  transfers between devices with their start and end apart: 4, of which 3 were waited for; matrix products, arithmetic and copies ran while one was open for 3% of the time, Pallas kernels for 0%

profile of v1, /device:TPU:16, one launch (start us, length us, event | category | flops | bytes accessed | tf_op | source)
XLA Modules:
  0.0 43.4 jit_solution(7934961820837312111)
XLA Ops:
  0.6 1.7 %shard_map.86 = (f32[25,8,128]{2,1,0:T(8,128)}, f32[25,8,128]{2,1,0:T(8,128)S(1)}) custom-call(f32[12,96,128]{2,1,0:T(8,128)} %refs_8_.3, f32[12,96,128]{2,1,0:T(8,128)} %refs_9_.3, f32[12,96,128]{2,1,0:T(8,128)} %refs_10_.3, f32[12,96,128]{2,1,0:T(8,128)} %refs_11_.3, f32[12,96,128]{2,1,0:T(8,128)} %refs_8_.3, f32[12,96,128]{2,1,0:T(8,128)} %refs_9_.3, ...), custom_call_target="tpu_custom_call" | custom-call | tf_op jit(solution)/shard_map/pallas_call | solution.py:433
  2.3 1.7 %collective-permute-start.8 = (f32[25,8,128]{2,1,0:T(8,128)}, f32[25,8,128]{2,1,0:T(8,128)S(1)}, u32[]{:S(2)}, u32[]{:S(2)}) collective-permute-start(f32[25,8,128]{2,1,0:T(8,128)} %get-tuple-element.24), channel_id=1, source_target_pairs={{0,1},{1,0},{2,3},{3,2},{4,5},{5,4},{6,7},{7,6},{8,9},{9,8},{10,11... | collective-permute-start | bytes 307208 | tf_op jit(solution)/shard_map/ppermute | solution.py:445
  4.0 1.2 %slice.3 = s32[1]{0:T(128)} slice(s32[1024]{0:T(1024)} %refs_0_.5), slice={[0:1]} | slice | bytes 8 | tf_op jit(solution)/shard_map/slice | solution.py:442
  7.8 6.7 %conditional.1 = (f32[25,8,128]{2,1,0:T(8,128)}) conditional(s32[]{:T(128)} %clamp.3, f32[25,8,128]{2,1,0:T(8,128)S(1)} %get-tuple-element.25, f32[25,8,128]{2,1,0:T(8,128)S(1)} %get-tuple-element.25, f32[25,8,128]{2,1,0:T(8,128)S(1)} %get-tuple-element.25, f32[25,8,128]{2,1,0:T(8,128)S(1)} %get-tuple-element.25, ...), branch_computations={%region_0.1_spmd, %region_1.2_spmd, %region_2.3_spmd, %region_3.4_... | conditional | bytes 409648 | solution.py:452
  7.8 1.9 %collective-permute-start = (f32[25,8,128]{2,1,0:T(8,128)S(1)}, f32[25,8,128]{2,1,0:T(8,128)}, u32[]{:S(2)}, u32[]{:S(2)}) collective-permute-start(f32[25,8,128]{2,1,0:T(8,128)S(1)} %param), channel_id=1, source_target_pairs={{1,2},{2,1},{5,6},{6,5},{9,10},{10,9},{13,14},{14,13},{17,18},{18,... | collective-permute-start | bytes 307208 | tf_op jit(solution)/shard_map/cond/branch_0_fun/ppermute | solution.py:450
  9.7 4.7 %collective-permute-done = f32[25,8,128]{2,1,0:T(8,128)} collective-permute-done((f32[25,8,128]{2,1,0:T(8,128)S(1)}, f32[25,8,128]{2,1,0:T(8,128)}, u32[]{:S(2)}, u32[]{:S(2)}) %collective-permute-start) | collective-permute-done | bytes 102432 | tf_op jit(solution)/shard_map/cond/branch_0_fun/ppermute | solution.py:450
  14.5 0.0 collective-permute-done.8.refs_6_.refs_1_
  14.5 0.0 copy-start
  14.5 0.6 %copy-done = f32[25,8,128]{2,1,0:T(8,128)} copy-done((f32[25,8,128]{2,1,0:T(8,128)}, f32[25,8,128]{2,1,0:T(8,128)S(1)}, u32[]{:S(2)}) %copy-start) | copy-done | bytes 102424
  15.1 3.5 %shard_map.87 = (f32[49,16,128]{2,1,0:T(8,128)}, f32[50,8,128]{2,1,0:T(8,128)}, f32[50,8,128]{2,1,0:T(8,128)}) custom-call(f32[12,96,128]{2,1,0:T(8,128)} %refs_8_.3, f32[12,96,128]{2,1,0:T(8,128)} %refs_9_.3, f32[12,96,128]{2,1,0:T(8,128)} %refs_10_.3, f32[12,96,128]{2,1,0:T(8,128)} %refs_11_.3, s32[96,128]{1,0:T(8,128)} %refs_6_.3, s32[96,128]{1,0:T(8,128)} %refs_7_.3, ...), custom_call_target="tpu_custom_call" | custom-call | tf_op jit(solution)/shard_map/pallas_call | solution.py:456
  18.6 0.5 %collective-permute-start.9 = (f32[50,8,128]{2,1,0:T(8,128)}, f32[50,8,128]{2,1,0:T(8,128)S(1)}, u32[]{:S(2)}, u32[]{:S(2)}) collective-permute-start(f32[50,8,128]{2,1,0:T(8,128)} %get-tuple-element.26), channel_id=1, source_target_pairs={{4,0},{8,4},{12,8},{16,12},{20,16},{24,20},{28,24},{0,28},{5,1},{9... | collective-permute-start | bytes 614408 | tf_op jit(solution)/shard_map/ppermute | solution.py:464
  19.0 0.1 collective-permute-start.10
  19.1 5.3 %collective-permute-done.9.refs_3_ = f32[50,8,128]{2,1,0:T(8,128)S(1)} collective-permute-done((f32[50,8,128]{2,1,0:T(8,128)}, f32[50,8,128]{2,1,0:T(8,128)S(1)}, u32[]{:S(2)}, u32[]{:S(2)}) %collective-permute-start.9) | collective-permute-done | bytes 204832 | tf_op jit(solution)/shard_map/ppermute | solution.py:464
  24.4 0.0 copy-start.1
  24.4 2.7 %collective-permute-done.10.refs_4_ = f32[50,8,128]{2,1,0:T(8,128)S(1)} collective-permute-done((f32[50,8,128]{2,1,0:T(8,128)}, f32[50,8,128]{2,1,0:T(8,128)S(1)}, u32[]{:S(2)}, u32[]{:S(2)}) %collective-permute-start.10) | collective-permute-done | bytes 204832 | tf_op jit(solution)/shard_map/ppermute | solution.py:463
  27.2 0.0 copy-start.2
  27.2 0.0 copy-done.1
  27.2 0.7 %copy-done.2 = f32[50,8,128]{2,1,0:T(8,128)} copy-done((f32[50,8,128]{2,1,0:T(8,128)}, f32[50,8,128]{2,1,0:T(8,128)S(1)}, u32[]{:S(2)}) %copy-start.2) | copy-done | bytes 204824
  27.9 15.5 %shard_map.88 = (f32[12,96,128]{2,1,0:T(8,128)}, f32[12,96,128]{2,1,0:T(8,128)}) custom-call(s32[1024]{0:T(1024)} %refs_0_.5, f32[25,8,128]{2,1,0:T(8,128)} %copy-done, f32[25,8,128]{2,1,0:T(8,128)} %get-tuple-element.29.refs_7_.refs_2_, f32[50,8,128]{2,1,0:T(8,128)} %copy-done.1, f32[50,8,128]{2,1,0:T(8,128)} %copy-done.2, ...), custom_call_target="tpu_custom_call" | custom-call | tf_op jit(solution)/shard_map/pallas_call | solution.py:468
Async XLA Ops:
  2.3 12.2 %collective-permute-start.8 = (f32[25,8,128]{2,1,0:T(8,128)}, f32[25,8,128]{2,1,0:T(8,128)S(1)}, u32[]{:S(2)}, u32[]{:S(2)}) collective-permute-start(f32[25,8,128]{2,1,0:T(8,128)} %get-tuple-element.24), channel_id=1, source_target_pairs={{0,1},{1,0},{2,3},{3,2},{4,5},{5,4},{6,7},{7,6},{8,9},{9,8},{10,11... | collective-permute-start | bytes 307208 | tf_op jit(solution)/shard_map/ppermute | solution.py:445
  7.8 6.7 %collective-permute-start = (f32[25,8,128]{2,1,0:T(8,128)S(1)}, f32[25,8,128]{2,1,0:T(8,128)}, u32[]{:S(2)}, u32[]{:S(2)}) collective-permute-start(f32[25,8,128]{2,1,0:T(8,128)S(1)} %param), channel_id=1, source_target_pairs={{1,2},{2,1},{5,6},{6,5},{9,10},{10,9},{13,14},{14,13},{17,18},{18,... | collective-permute-start | bytes 307208 | tf_op jit(solution)/shard_map/cond/branch_0_fun/ppermute | solution.py:450
  14.5 0.6 %copy-start = (f32[25,8,128]{2,1,0:T(8,128)}, f32[25,8,128]{2,1,0:T(8,128)S(1)}, u32[]{:S(2)}) copy-start(f32[25,8,128]{2,1,0:T(8,128)S(1)} %collective-permute-done.8.refs_6_.refs_1_) | copy-start | bytes 307204
  18.6 5.9 %collective-permute-start.9 = (f32[50,8,128]{2,1,0:T(8,128)}, f32[50,8,128]{2,1,0:T(8,128)S(1)}, u32[]{:S(2)}, u32[]{:S(2)}) collective-permute-start(f32[50,8,128]{2,1,0:T(8,128)} %get-tuple-element.26), channel_id=1, source_target_pairs={{4,0},{8,4},{12,8},{16,12},{20,16},{24,20},{28,24},{0,28},{5,1},{9... | collective-permute-start | bytes 614408 | tf_op jit(solution)/shard_map/ppermute | solution.py:464
  19.0 8.1 %collective-permute-start.10 = (f32[50,8,128]{2,1,0:T(8,128)}, f32[50,8,128]{2,1,0:T(8,128)S(1)}, u32[]{:S(2)}, u32[]{:S(2)}) collective-permute-start(f32[50,8,128]{2,1,0:T(8,128)} %get-tuple-element.27), channel_id=1, source_target_pairs={{0,4},{4,8},{8,12},{12,16},{16,20},{20,24},{24,28},{28,0},{1,5},{5... | collective-permute-start | bytes 614408 | tf_op jit(solution)/shard_map/ppermute | solution.py:463
  24.4 2.7 %copy-start.1 = (f32[50,8,128]{2,1,0:T(8,128)}, f32[50,8,128]{2,1,0:T(8,128)S(1)}, u32[]{:S(2)}) copy-start(f32[50,8,128]{2,1,0:T(8,128)S(1)} %collective-permute-done.9.refs_3_) | copy-start | bytes 614404
  27.2 0.7 %copy-start.2 = (f32[50,8,128]{2,1,0:T(8,128)}, f32[50,8,128]{2,1,0:T(8,128)S(1)}, u32[]{:S(2)}) copy-start(f32[50,8,128]{2,1,0:T(8,128)S(1)} %collective-permute-done.10.refs_4_) | copy-start | bytes 614404
